TPU v7x, 32 devices: a whole 2x2x4 slice. The times are simulated.
32 devices in a mesh: row: 4 (over y, x), col: 8 (over z, core).
Axes of the slice: x: 2, y: 2, z: 4, core: 2. Of those that a mesh axis runs over, the one named last changes fastest.
Arguments:
- matrix: float32 [16384, 16384], P('row', 'col'), may hold values from -85 to 723.7488, as said below
Outputs:
- reduced: float32 [16384, 16384], P('row', 'col')
Inputs may be any that keep to these rules, and one draw needn't show every extreme that they name: matrix is symmetric; entry (64 + j, j) and its mirror exceed the other entries of their columns many times over, so that the leading entry of every panel column stays positive through the reflections.
All inputs are finite; a program needn't handle non-finite values.
Results may differ from a plain program's by a relative error of at most 0.00011.
Values sent between devices are 32-bit elements; how exact they have to be, the bound alone decides.
A program may use at most 192 MiB of HBM per device.

v0:
```python
import jax
import jax.numpy as jnp
from jax import lax
from jax.sharding import PartitionSpec as P

B = 64


highest = lax.Precision.HIGHEST


def spread(block, axis, source):
    block = jnp.where(lax.axis_index(axis) == source, block, jnp.zeros_like(block))
    return lax.psum(block, axis)


def across(left, right):
    return lax.dot_general(left, right, (((0,), (0,)), ((), ())), precision=highest)


def outer_rows(left, right):
    return lax.dot_general(left, right, (((1,), (1,)), ((), ())), precision=highest)


def reflect_loop(panel_cols, rows_all, combine):

    def reflect_step(index, state):
        working, vectors = state
        column = lax.dynamic_slice_in_dim(working, index, 1, 1)[:, 0]
        masked = jnp.where(rows_all >= index, column, jnp.zeros_like(column))
        chosen = (rows_all == index).astype(working.dtype)
        totals, pivot_row = combine(
            (
                jnp.dot(masked, working, precision=highest),
                jnp.dot(chosen, working, precision=highest),
            )
        )
        square_sum = totals[index]
        leading = pivot_row[index]
        norm_value = jnp.sqrt(square_sum)
        vector = masked + norm_value * chosen
        tau_value = 2.0 / (2.0 * square_sum + 2.0 * leading * norm_value)
        working = working - tau_value * jnp.outer(vector, totals + norm_value * pivot_row)
        column_mark = (jnp.arange(B, dtype=jnp.int32) == index).astype(working.dtype)
        vectors = vectors + jnp.outer(vector, column_mark)
        return (working, vectors)

    start = (panel_cols, jnp.zeros_like(panel_cols))
    return lax.fori_loop(0, B, reflect_step, start)[1]


def row_combine(pair):
    return lax.psum((pair[0], pair[1]), "row")


def compact_factor(gram_matrix):
    width = gram_matrix.shape[0]
    diag_half = 0.5 * jnp.diag(gram_matrix)
    inverse_diag = 1.0 / diag_half
    nilpotent = -(jnp.triu(gram_matrix, 1) * inverse_diag[:, None])
    identity = jnp.eye(width, dtype=gram_matrix.dtype)
    product = identity + nilpotent
    power = nilpotent
    reach = 2
    while reach < width:
        power = jnp.dot(power, power, precision=highest)
        product = jnp.dot(product, identity + power, precision=highest)
        reach = reach * 2
    return product * inverse_diag[None, :]


def on_device(matrix):
    rows_dev, cols_dev = matrix.shape
    row_pos = lax.axis_index("row")
    col_pos = lax.axis_index("col")
    panel_cols = spread(matrix[:, :B], "col", 0)
    rows_all = row_pos * rows_dev + jnp.arange(rows_dev, dtype=jnp.int32) - B
    vectors_rows = reflect_loop(panel_cols, rows_all, row_combine)
    owner = col_pos * cols_dev // rows_dev
    offset = col_pos * cols_dev % rows_dev
    vectors_cols = spread(lax.dynamic_slice_in_dim(vectors_rows, offset, cols_dev, 0), "row", owner)
    part_rows = jnp.dot(matrix, vectors_cols, precision=highest)
    image_rows = lax.psum(part_rows, "col")
    image_cols = lax.psum(across(matrix, vectors_rows), "row")
    core, gram_matrix = lax.psum(
        (across(vectors_rows, image_rows), across(vectors_rows, vectors_rows)), "row"
    )
    compact = compact_factor(gram_matrix)
    middle = jnp.dot(jnp.dot(compact.T, core, precision=highest), compact, precision=highest)
    update_rows = jnp.dot(image_rows, compact, precision=highest) - 0.5 * jnp.dot(
        vectors_rows, middle, precision=highest
    )
    update_cols = jnp.dot(image_cols, compact, precision=highest) - 0.5 * jnp.dot(
        vectors_cols, middle, precision=highest
    )
    return matrix - outer_rows(vectors_rows, update_cols) - outer_rows(update_rows, vectors_cols)


def solution(mesh):
    placed = (P("row", "col"),)
    return jax.shard_map(
        on_device, mesh=mesh, in_specs=placed, out_specs=P("row", "col"), check_vma=False
    )
```

profile of v0, /device:TPU:7, one launch (start us, length us, event | category | flops | bytes accessed | tf_op | source)
XLA Modules:
  0.0 1663.6 jit_solution(16801113258569082386)
XLA Ops:
  10.0 58.2 %all-reduce.9.cloned.1.call-done = f32[4096,64]{0,1:T(8,128)} async-done(((f32[4096,64]{0,1:T(8,128)}), f32[4096,64]{0,1:T(8,128)}) %all-reduce.9.cloned.1.call-update) | async-done | bytes 1048592 | tf_op jit(solution)/shard_map/psum | solution.py:14
  68.2 1185.1 %while.16 = (s32[]{:T(128)}, f32[4096,64]{0,1:T(8,128)}, f32[4096,64]{0,1:T(8,128)S(1)}, s32[]{:T(128)}, s32[]{:T(128)}, /*index=5*/s32[]{:T(128)}, f32[]{:T(128)}, f32[1]{0:T(128)}) while((s32[]{:T(128)}, f32[4096,64]{0,1:T(8,128)}, f32[4096,64]{0,1:T(8,128)S(1)}, s32[]{:T(128)}, s32[]{:T(128)}, /*index=5*/s32[]{:T(128)}, ...), condition=%wide.region_4.5_spmd.clone, body=%wide.region_1.4_spmd.clone.sunk | while | flops 7930248 | bytes 6483195 | solution.py:49
  91.0 7.1 all-reduce.4
  127.6 7.9 all-reduce.4
  165.0 7.1 all-reduce.4
  201.6 7.9 all-reduce.4
  239.0 7.4 all-reduce.4
  275.6 7.9 all-reduce.4
  313.3 7.1 all-reduce.4
  349.9 7.6 all-reduce.4
  387.3 7.1 all-reduce.4
  423.9 7.6 all-reduce.4
  443.4 6.4 all-reduce.4
  461.6 6.8 all-reduce.4
  498.2 7.3 all-reduce.4
  517.4 6.4 all-reduce.4
  535.6 6.8 all-reduce.4
  572.2 7.3 all-reduce.4
  591.4 6.4 all-reduce.4
  609.7 6.7 all-reduce.4
  646.3 7.5 all-reduce.4
  665.6 6.2 all-reduce.4
  683.7 6.7 all-reduce.4
  720.3 7.5 all-reduce.4
  739.6 6.2 all-reduce.4
  757.7 6.7 all-reduce.4
  794.3 7.5 all-reduce.4
  813.6 6.3 all-reduce.4
  831.8 6.6 all-reduce.4
  850.2 6.3 all-reduce.4
  868.4 7.7 all-reduce.4
  905.8 6.9 all-reduce.4
  942.4 7.7 all-reduce.4
  979.8 6.9 all-reduce.4
  1016.4 8.0 all-reduce.4
  1053.8 7.4 all-reduce.4
  1090.6 7.7 all-reduce.4
  1127.8 7.4 all-reduce.4
  1164.6 7.7 all-reduce.4
  1201.9 7.3 all-reduce.4
  1238.6 7.7 all-reduce.4
  1253.3 24.8 %convolution_bitcast_fusion.3 = f32[2048,64]{0,1:T(8,128)} fusion(f32[4096,64]{0,1:T(8,128)S(1)} %get-tuple-element.84, f32[4096,2048]{1,0:T(8,128)} %param.3), kind=kOutput, calls=%fused_computation.22 | convolution fusion | flops 6442450944 | bytes 35127296 | tf_op jit(solution)/shard_map/dot_general | solution.py:18
  1279.2 180.8 %all-reduce.13.cloned.1.call-done = (f32[2048,64]{0,1:T(8,128)}, f32[2048,64]{0,1:T(8,128)}) async-done(((f32[2048,64]{0,1:T(8,128)}, f32[2048,64]{0,1:T(8,128)}), (f32[2048,64]{0,1:T(8,128)}, f32[2048,64]{0,1:T(8,128)})) %all-reduce.13.cloned.1.call-update) | async-done | bytes 1048592 | tf_op jit(solution)/shard_map/psum | solution.py:84
  1460.0 38.4 %convolution_bitcast_fusion.2 = f32[4096,64]{0,1:T(8,128)} fusion(f32[2048,64]{0,1:T(8,128)} %get-tuple-element.116, f32[4096,2048]{1,0:T(8,128)} %param.3), kind=kOutput, calls=%fused_computation.19 | convolution fusion | flops 6442450944 | bytes 35127296 | tf_op jit(solution)/shard_map/dot_general | solution.py:82
  1499.3 57.1 %all-reduce.11.cloned.1.call-done = f32[4096,64]{0,1:T(8,128)} async-done(((f32[4096,64]{0,1:T(8,128)}), f32[4096,64]{0,1:T(8,128)}) %all-reduce.11.cloned.1.call-update) | async-done | bytes 1048592 | tf_op jit(solution)/shard_map/psum | solution.py:83
  1558.6 11.3 all-reduce.1
  1584.8 30.8 %fusion.26 = f32[4096,2048]{1,0:T(8,128)} fusion(f32[4096,64]{0,1:T(8,128)S(1)} %get-tuple-element.84, f32[2048,64]{1,0:T(8,128)S(1)} %fusion.6), kind=kOutput, calls=%fused_computation.56 | convolution fusion | flops 6442450944 | bytes 35127296 | tf_op jit(solution)/shard_map/dot_general | solution.py:22
  1615.7 41.2 %subtract_subtract_fusion = f32[4096,2048]{1,0:T(8,128)} fusion(f32[4096,2048]{1,0:T(8,128)} %param.3, f32[4096,2048]{1,0:T(8,128)} %fusion.26, f32[4096,64]{1,0:T(8,128)S(1)} %fusion.5, f32[2048,64]{0,1:T(8,128)} %get-tuple-element.116), kind=kOutput, calls=%fused_computation.16 | convolution fusion | flops 6459228160 | bytes 102236160 | tf_op jit(solution)/shard_map/dot_general | solution.py:22
  (957 shorter events, 795.6 us)
Async XLA Ops:
  6.5 61.7 %all-reduce.9.cloned.1.call-start = ((), (), s32[]{:S(2)}) async-start(), calls=%async_computation | async-start | bytes 2097152 | tf_op jit(solution)/shard_map/psum | solution.py:14
  9.9 1450.0 %all-reduce.13.cloned.1.call-start = ((), (), s32[]{:S(2)}) async-start(), calls=%async_computation.2 | async-start | bytes 2097152 | tf_op jit(solution)/shard_map/psum | solution.py:84
  1279.0 277.4 %all-reduce.11.cloned.1.call-start = ((), (), s32[]{:S(2)}) async-start(), calls=%async_computation.1 | async-start | bytes 2097152 | tf_op jit(solution)/shard_map/psum | solution.py:83
  1460.0 113.0 %copy-start.1 = (f32[2048,64]{0,1:T(8,128)S(1)}, f32[2048,64]{0,1:T(8,128)}, u32[]{:S(2)}) copy-start(f32[2048,64]{0,1:T(8,128)} %get-tuple-element.115) | copy-start | bytes 1572868
  1460.0 114.8 %copy-start = (f32[2048,64]{0,1:T(8,128)S(1)}, f32[2048,64]{0,1:T(8,128)}, u32[]{:S(2)}) copy-start(f32[2048,64]{0,1:T(8,128)} %get-tuple-element.116) | copy-start | bytes 1572868
Sparse Core Ops, SparseCore 0:
  10.0 58.1 all-reduce.8
  1279.1 180.8 all-reduce.12
  1498.5 57.8 all-reduce.10
where the time goes:
time: 1690 us; the launch traced here: 1660 us
  blocking collectives  438 us (26%)
  matrix products  405 us (24%)
  waiting for transfers between devices  296 us (18%)
  other arithmetic  239 us (14%)
  local copies, waits for them, and re-layouts  139 us (8%)
  loops' own time  133 us (8%)
    psum x64, blocking collectives, row_combine(): return lax.psum((pair[0], pair[1]), 'row')  426 us
    psum x1, waiting for transfers between devices, on_device(): image_cols = lax.psum(across(matrix, vectors_rows), 'row')  181 us
    add x64, other arithmetic, reflect_step(): vectors = vectors + jnp.outer(vector, column_mark)  174 us
    dot_general x64, matrix products, reflect_step(): jnp.dot(masked, working, precision=highest)  137 us
    another operation x1, loops' own time, reflect_loop(): return lax.fori_loop(0, B, reflect_step, start)[1]  133 us
    dot_general x64, matrix products, reflect_step(): jnp.dot(chosen, working, precision=highest)  116 us
    dot_general x2, matrix products, outer_rows(): lax.dot_general(left, right, (((1,), (1,)), ((), ())), precision=highest)  72.1 us
    add x64, other arithmetic, reflect_step(): vector = masked + norm_value * chosen  60.4 us
  transfers between devices with their start and end apart: 3, of which 3 were waited for; matrix products, arithmetic and copies ran while one was open for 0% of the time, Pallas kernels for 0%

commit v1 on v0

v1 whole, which is shorter than its diff:
```python
import jax
import jax.numpy as jnp
from jax import lax
from jax.experimental import pallas as pl
from jax.experimental.pallas import tpu as pltpu
from jax.sharding import PartitionSpec as P

B = 64

highest = lax.Precision.HIGHEST
high = lax.Precision.HIGH


def dot(left, right, dims, precision=high):
    return lax.dot_general(
        left, right, (dims, ((), ())), precision=precision, preferred_element_type=jnp.float32
    )


def factor_kernel(small_ref, upper_ref, inner_ref):
    lane = lax.broadcasted_iota(jnp.int32, (B, 2 * B), 1)
    sub = lax.broadcasted_iota(jnp.int32, (B, 2 * B), 0)
    left = lane < B
    shifted_eye = (lane == sub + B).astype(jnp.float32)
    both = small_ref[...]
    swapped = jnp.concatenate([both[:, B:], both[:, :B]], axis=1)
    grams = jnp.where(left, both, shifted_eye)
    pivots = jnp.where(left, swapped, shifted_eye)
    left_row = left[:1]
    factors = jnp.zeros((B, 2 * B), jnp.float32)
    for j in range(B):
        here = sub == j
        row = grams[j : j + 1, :]
        scale = lax.rsqrt(row[:, j : j + 1])
        scaled = row * scale
        grams = grams - (grams[:, j : j + 1] * scale) * scaled
        factors = jnp.where(here, scaled, factors)
        line = pivots[j : j + 1, :] + jnp.where(left_row, scaled, 0.0)
        line = line / line[:, j : j + 1]
        pivots = jnp.where(here, line, pivots - pivots[:, j : j + 1] * line)
    upper = (lane >= sub)[:, :B]
    upper_ref[...] = jnp.where(upper, factors[:, :B], 0.0)
    inner_ref[...] = dot(factors[:, B:], pivots[:, B:], ((0,), (1,)), highest)


def factor(small):
    shape = jax.ShapeDtypeStruct((B, B), jnp.float32)
    return pl.pallas_call(
        factor_kernel,
        out_shape=(shape, shape),
        cost_estimate=pl.CostEstimate(flops=30_000_000, bytes_accessed=65536, transcendentals=0),
    )(small)


def on_device(matrix):
    rows_dev, cols_dev = matrix.shape
    row_pos = lax.axis_index("row")
    col_pos = lax.axis_index("col")
    first_row = row_pos == 0
    first_col = col_pos == 0
    strip_rows = lax.psum(jnp.where(first_col, matrix[:, : 2 * B], 0.0), "col")
    strip_cols = lax.psum(jnp.where(first_row, matrix[: 2 * B, :], 0.0), "row")
    row_ids = row_pos * rows_dev + jnp.arange(rows_dev, dtype=jnp.int32)
    col_ids = col_pos * cols_dev + jnp.arange(cols_dev, dtype=jnp.int32)
    panel_rows = jnp.where((row_ids >= B)[:, None], strip_rows[:, :B], 0.0)
    panel_cols = jnp.where((col_ids >= B)[None, :], strip_cols[:B, :], 0.0)
    top = jnp.where(first_row, strip_rows[B : 2 * B, :], 0.0)
    gram = dot(panel_rows, panel_rows, ((0,), (0,)), highest)
    small = lax.psum(jnp.concatenate([gram, top], axis=1), "row")
    part_rows = dot(matrix, panel_cols, ((1,), (1,)))
    part_cols = dot(panel_rows, matrix, ((0,), (0,)))
    image_rows = lax.psum(part_rows, "col")
    image_cols = lax.psum(part_cols, "row")
    core_part = dot(panel_rows, part_rows, ((0,), (0,)))
    edge_part = jnp.where(first_row, part_rows[B : 2 * B, :], 0.0)
    cores = lax.psum(jnp.concatenate([core_part, edge_part], axis=1), ("row", "col"))
    upper, inner = factor(small[:, : 2 * B])
    corner = small[:, 2 * B :]
    edge = dot(upper, cores[:, B:], ((0,), (0,)), highest)
    core = cores[:, :B] + edge + edge.T + dot(
        upper, dot(corner, upper, ((1,), (0,)), highest), ((0,), (0,)), highest
    )
    middle = 0.5 * dot(inner, dot(core, inner, ((1,), (0,)), highest), ((0,), (0,)), highest)
    pad_rows = jnp.where(first_row, upper, 0.0)
    pad_cols = jnp.where(first_col, upper.T, 0.0)
    basis_rows = panel_rows.at[B : 2 * B, :].add(pad_rows)
    basis_cols = panel_cols.at[:, B : 2 * B].add(pad_cols)
    image_rows = image_rows + dot(strip_rows[:, B:], upper, ((1,), (0,)))
    image_cols = image_cols + dot(upper, strip_cols[B:, :], ((0,), (0,)))
    update_rows = dot(image_rows, inner, ((1,), (0,))) - dot(basis_rows, middle, ((1,), (0,)))
    update_cols = dot(inner, image_cols, ((0,), (0,))) - dot(middle, basis_cols, ((0,), (0,)))
    lefts = jnp.concatenate([basis_rows, update_rows], axis=1)
    rights = jnp.concatenate([update_cols, basis_cols], axis=0)
    return matrix - dot(lefts, rights, ((1,), (0,)))


def solution(mesh):
    placed = (P("row", "col"),)
    return jax.shard_map(
        on_device, mesh=mesh, in_specs=placed, out_specs=P("row", "col"), check_vma=False
    )
```

time: 1690 us -> 378 us (0.22); the launches traced: 1660 us -> 375 us
  blocking collectives: 438 us -> 50.5 us
  matrix products: 405 us -> 89.6 us
  other arithmetic: 239 us -> 12.3 us
  local copies, waits for them, and re-layouts: 139 us -> 4.32 us
  loops' own time: 133 us -> 0 us
  waiting for transfers between devices: 296 us -> 197 us
    psum x65 -> x2, blocking collectives: 438 us -> 50.5 us  [the longest x1 39.6 us: on_device(): lax.psum(jnp.concatenate([core_part, edge_part], axis=1), ('row', 'col'))]
    dot_general x150 -> x16, matrix products: 405 us -> 89.6 us  [dot(): lax.dot_general(left, right, (dims, ((), ())), precision=precision, prefe...]
    add x192 -> x0, other arithmetic: 234 us -> none  [the longest x64 174 us: reflect_step(): vectors = vectors + jnp.outer(vector, column_mark)]
    psum x2, waiting for transfers between devices: 239 us -> 97 us  [the longest x1 51 us: on_device(): strip_cols = lax.psum(jnp.where(first_row, matrix[:2 * B, :], 0.0), 'row')]
    dynamic_slice x192 -> x0, local copies, waits for them, and re-layouts: 135 us -> none  [the longest x64 59.6 us: reflect_step(): column = lax.dynamic_slice_in_dim(working, index, 1, 1)[:, 0]]
    another operation x1 -> x0, loops' own time: 133 us -> none  [reflect_loop(): return lax.fori_loop(0, B, reflect_step, start)[1]]
    psum x1, waiting for transfers between devices: 57.1 us -> 99.4 us  [on_device(): image_rows = lax.psum(part_rows, 'col')]
  transfers between devices with their start and end apart: 3 -> 3, of which waited for: 3 -> 3; matrix products, arithmetic and copies ran while one was open for 0% -> 2% of each run, Pallas kernels for 0% -> 0%
where the time goes in v1:
time: 378 us; the launch traced here: 375 us
  waiting for transfers between devices  197 us (52%)
  matrix products  89.6 us (24%)
  blocking collectives  50.5 us (13%)
  between operations  13.3 us (4%)
  other arithmetic  12.3 us (3%)
  Pallas kernels  7.29 us (2%)
  local copies, waits for them, and re-layouts  4.32 us (1%)
    psum x1, waiting for transfers between devices, on_device(): image_rows = lax.psum(part_rows, 'col')  99.4 us
    dot_general x16, matrix products, dot(): lax.dot_general(left, right, (dims, ((), ())), precision=precision, prefe...  89.6 us
    psum x1, waiting for transfers between devices, on_device(): strip_cols = lax.psum(jnp.where(first_row, matrix[:2 * B, :], 0.0), 'row')  51 us
    psum x1, waiting for transfers between devices, on_device(): image_cols = lax.psum(part_cols, 'row')  46 us
    psum x1, blocking collectives, on_device(): lax.psum(jnp.concatenate([core_part, edge_part], axis=1), ('row', 'col'))  39.6 us
    psum x1, blocking collectives, on_device(): small = lax.psum(jnp.concatenate([gram, top], axis=1), 'row')  11 us
  transfers between devices with their start and end apart: 3, of which 3 were waited for; matrix products, arithmetic and copies ran while one was open for 2% of the time, Pallas kernels for 0%

profile of v1, /device:TPU:7, one launch (start us, length us, event | category | flops | bytes accessed | tf_op | source)
XLA Modules:
  0.0 374.8 jit_solution(10062248661178060421)
XLA Ops:
  6.5 0.0 all-reduce.5.cloned.1.call-start
  6.5 1.2 slice-done
  7.8 0.3 copy.5
  8.1 1.0 broadcast_select_fusion
  9.1 0.0 all-reduce.5.cloned.1.call-update
  9.2 3.0 slice_select_fusion.1
  12.2 51.0 %all-reduce.5.cloned.1.call-done = f32[128,2048]{0,1:T(8,128)} async-done(((f32[128,2048]{0,1:T(8,128)}), f32[128,2048]{0,1:T(8,128)}) %all-reduce.5.cloned.1.call-update) | async-done | bytes 1048592 | tf_op jit(solution)/shard_map/psum | solution.py:62
  63.3 1.6 slice_select_fusion.2
  64.8 21.4 %fusion.17 = f32[64,4096]{1,0:T(8,128)S(1)} fusion(f32[64,2048]{0,1:T(8,128)S(1)} %slice_select_fusion.2, f32[4096,2048]{1,0:T(8,128)} %param.5), kind=kOutput, calls=%fused_computation.38 | convolution fusion | flops 3221225472 | bytes 35127296 | tf_op jit(solution)/shard_map/dot_general | solution.py:15
  86.3 0.0 copy-start
  86.3 1.9 copy.3
  88.2 0.8 slice_select_fusion.3
  89.0 0.0 all-reduce.9.cloned.1.call-start
  89.0 0.7 all-reduce.9.cloned.1.call-update
  89.7 0.0 copy-done
  89.7 0.2 all-reduce.7.cloned.1.call-start
  90.0 0.7 compare_reduce_fusion
  90.6 99.4 %all-reduce.9.cloned.1.call-done = (f32[4096,64]{1,0:T(8,128)}, f32[4096,128]{1,0:T(8,128)}) async-done(((f32[4096,64]{1,0:T(8,128)}, f32[4096,128]{1,0:T(8,128)}), (f32[4096,64]{1,0:T(8,128)}, f32[4096,128]{1,0:T(8,128)})) %all-reduce.9.cloned.1.call-update) | async-done | bytes 3145744 | tf_op jit(solution)/shard_map/psum | solution.py:72
  190.0 0.8 slice_select_fusion.4
  190.8 3.7 slice_select_fusion
  194.5 0.0 copy-done.1
  194.5 1.8 fusion.19
  196.3 3.6 fusion.16
  199.9 17.4 %fusion.21 = f32[64,2048]{1,0:T(8,128)} fusion(f32[4096,64]{1,0:T(8,128)S(1)} %slice_select_fusion, f32[4096,2048]{1,0:T(8,128)} %param.5), kind=kOutput, calls=%fused_computation.42 | convolution fusion | flops 3221225472 | bytes 35127296 | tf_op jit(solution)/shard_map/dot_general | solution.py:15
  217.3 0.1 pad_maximum_fusion.1
  217.4 39.6 %psum.46 = f32[64,128]{1,0:T(8,128)S(1)} all-reduce(f32[64,128]{1,0:T(8,128)S(1)} %pad_maximum_fusion.1), channel_id=1, replica_groups=mesh['row'=4,'col'=8] {'row','col'}, use_global_device_ids=true, to_apply=%region_4.5 | all-reduce | flops 8192 | bytes 65536 | tf_op jit(solution)/shard_map/psum | solution.py:76
  256.9 0.1 pad_maximum_fusion
  257.0 11.0 %psum.43 = f32[64,192]{1,0:T(8,128)S(1)} all-reduce(f32[64,192]{1,0:T(8,128)S(1)} %pad_maximum_fusion), channel_id=1, replica_groups=mesh['row'=4,'col'=8] {'row'}, use_global_device_ids=true, to_apply=%region_1.2 | all-reduce | flops 12288 | bytes 98304 | tf_op jit(solution)/shard_map/psum | solution.py:69
  268.0 0.6 slice.91.small_ref
  268.6 7.3 %shard_map.17 = (f32[64,64]{1,0:T(8,128)}, f32[64,64]{1,0:T(8,128)}) custom-call(f32[64,128]{1,0:T(8,128)} %slice.91.small_ref), custom_call_target="tpu_custom_call" | custom-call | flops 30000000 | bytes 65536 | tf_op jit(solution)/shard_map/pallas_call | solution.py:48
  275.9 0.9 fusion.9
  276.8 4.8 %convolution_add_fusion = f32[4096,64]{1,0:T(8,128)} fusion(f32[4096,64]{1,0:T(8,128)} %get-tuple-element.33, f32[64,64]{1,0:T(8,128)} %get-tuple-element.31, f32[4096,128]{1,0:T(8,128)} %get-tuple-element.34), kind=kOutput, calls=%fused_computation.2 | convolution fusion | flops 100925440 | bytes 4210688 | tf_op jit(solution)/shard_map/dot_general | solution.py:15
  281.7 0.0 copy-done.4
  281.7 0.6 fusion.8
  282.3 0.3 fusion.11
  282.6 0.1 copy.4
  282.7 3.9 %fusion.18 = f32[4096,64]{1,0:T(8,128)} fusion(f32[4096,64]{1,0:T(8,128)} %convolution_add_fusion, f32[64,64]{1,0:T(8,128)S(1)} %copy-done.5), kind=kOutput, calls=%fused_computation.39 | convolution fusion | flops 100663296 | bytes 2113536 | tf_op jit(solution)/shard_map/dot_general | solution.py:15
  286.6 0.2 convolution_add_fusion.2
  286.8 0.2 fusion.20
  287.0 0.2 convolution_multiply_fusion
  287.2 0.0 all-reduce.7.cloned.1.call-update
  287.3 1.5 fusion.22
  288.8 0.1 copy-done.2
  288.9 2.3 convolution_subtract_fusion.1
  291.3 46.0 %all-reduce.7.cloned.1.call-done = f32[64,2048]{1,0:T(8,128)} async-done(((f32[64,2048]{1,0:T(8,128)}), f32[64,2048]{1,0:T(8,128)}) %all-reduce.7.cloned.1.call-update) | async-done | bytes 524304 | tf_op jit(solution)/shard_map/psum | solution.py:73
  337.3 2.3 convolution_add_fusion.1
  339.6 1.0 convolution_subtract_fusion.2
  340.6 27.7 %convolution_subtract_fusion = f32[4096,2048]{1,0:T(8,128)} fusion(f32[4096,2048]{1,0:T(8,128)} %param.5, f32[4096,64]{1,0:T(8,128)} %convolution_subtract_fusion.1, f32[4096,64]{1,0:T(8,128)S(1)} %fusion.14, f32[64,2048]{0,1:T(8,128)S(1)} %fusion.8, f32[64,2048]{0,1:T(8,128)S(1)} %convolution_subtract_fusion.2), kind=kOutput, calls=%fused_computation | convolution fusion | flops 6451625984 | bytes 70254592 | tf_op jit(solution)/shard_map/dot_general | solution.py:15
  (11 shorter events, 0.0 us)
Async XLA Ops:
  6.5 1.2 slice-start
  6.5 56.7 %all-reduce.5.cloned.1.call-start = ((), (), s32[]{:S(2)}) async-start(), calls=%async_computation | async-start | bytes 2097152 | tf_op jit(solution)/shard_map/psum | solution.py:62
  86.3 3.4 copy-start
  89.0 101.0 %all-reduce.9.cloned.1.call-start = ((), (), s32[]{:S(2)}) async-start(), calls=%async_computation.2 | async-start | bytes 8388608 | tf_op jit(solution)/shard_map/psum | solution.py:72
  89.7 247.5 %all-reduce.7.cloned.1.call-start = ((), (), s32[]{:S(2)}) async-start(), calls=%async_computation.1 | async-start | bytes 1048576 | tf_op jit(solution)/shard_map/psum | solution.py:73
  190.8 3.7 copy-start.1
  276.8 4.9 %copy-start.4 = (f32[64,64]{1,0:T(8,128)S(1)}, f32[64,64]{1,0:T(8,128)}, u32[]{:S(2)}) copy-start(f32[64,64]{1,0:T(8,128)} %get-tuple-element.31) | copy-start | bytes 49156
  276.8 5.8 %copy-start.5 = (f32[64,64]{1,0:T(8,128)S(1)}, f32[64,64]{1,0:T(8,128)}, u32[]{:S(2)}) copy-start(f32[64,64]{1,0:T(8,128)} %get-tuple-element.32) | copy-start | bytes 49156
  287.2 1.7 copy-start.2
  337.3 2.3 copy-start.3
Sparse Core Ops, SparseCore 0:
  10.4 52.8 all-reduce.4
  92.2 97.7 all-reduce.8
  287.4 49.8 all-reduce.6

commit v2 on v1

v2 whole, which is shorter than its diff:
```python
import functools
import math

import jax
import jax.numpy as jnp
from jax import lax
from jax.experimental import pallas as pl
from jax.experimental.pallas import tpu as pltpu
from jax.sharding import PartitionSpec as P

B = 64

highest = lax.Precision.HIGHEST
high = lax.Precision.HIGH


def dot(left, right, dims, precision=high):
    return lax.dot_general(
        left, right, (dims, ((), ())), precision=precision, preferred_element_type=jnp.float32
    )


def factor_kernel(small_ref, upper_ref, inner_ref):
    lane = lax.broadcasted_iota(jnp.int32, (B, 2 * B), 1)
    sub = lax.broadcasted_iota(jnp.int32, (B, 2 * B), 0)
    left = lane < B
    shifted_eye = (lane == sub + B).astype(jnp.float32)
    both = small_ref[...]
    swapped = jnp.concatenate([both[:, B:], both[:, :B]], axis=1)
    grams = jnp.where(left, both, shifted_eye)
    pivots = jnp.where(left, swapped, shifted_eye)
    left_row = left[:1]
    factors = jnp.zeros((B, 2 * B), jnp.float32)
    for j in range(B):
        here = sub == j
        row = grams[j : j + 1, :]
        scale = lax.rsqrt(row[:, j : j + 1])
        scaled = row * scale
        grams = grams - (grams[:, j : j + 1] * scale) * scaled
        factors = jnp.where(here, scaled, factors)
        line = pivots[j : j + 1, :] + jnp.where(left_row, scaled, 0.0)
        line = line / line[:, j : j + 1]
        pivots = jnp.where(here, line, pivots - pivots[:, j : j + 1] * line)
    upper = (lane >= sub)[:, :B]
    upper_ref[...] = jnp.where(upper, factors[:, :B], 0.0)
    inner_ref[...] = dot(factors[:, B:], pivots[:, B:], ((0,), (1,)), highest)


def factor(small):
    shape = jax.ShapeDtypeStruct((B, B), jnp.float32)
    return pl.pallas_call(
        factor_kernel,
        out_shape=(shape, shape),
        cost_estimate=pl.CostEstimate(flops=30_000_000, bytes_accessed=65536, transcendentals=0),
    )(small)


MESH = pl.DeviceIdType.MESH


def exchange_kernel(n_row, n_col, blocks, pieces, own, *refs):
    if own:
        part_ref, total_ref, wide_ref, small_ref, *refs = refs
        other_ref = None
    else:
        part_ref, other_ref, total_ref, wide_ref, small_ref, *refs = refs
    slots, smalls, rs_send, rs_recv, ag_send, ag_recv, sm_send, sm_recv, ch_send, ch_recv = refs
    row = lax.axis_index("row")
    col = lax.axis_index("col")
    width = part_ref.shape[1]
    lane_parts = math.gcd(n_row, width // 128)
    sub_size = B * lane_parts // n_row
    lane_size = width // lane_parts

    barrier = pltpu.get_barrier_semaphore()
    for k in range(1, n_row):
        pl.semaphore_signal(
            barrier, inc=1, device_id={"row": lax.rem(row + k, n_row)}, device_id_type=MESH
        )
    for k in range(1, n_col):
        pl.semaphore_signal(
            barrier, inc=1, device_id={"col": lax.rem(col + k, n_col)}, device_id_type=MESH
        )
    pl.semaphore_wait(barrier, n_row + n_col - 2)

    def chunk(ref, j):
        sub = pl.multiple_of((j // lane_parts) * sub_size, sub_size)
        lanes = pl.multiple_of(lax.rem(j, lane_parts) * lane_size, lane_size)
        return ref.at[pl.ds(sub, sub_size), pl.ds(lanes, lane_size)]

    scatters = []
    for k in range(1, n_row):
        peer = lax.rem(row + k, n_row)
        copy = pltpu.make_async_remote_copy(
            src_ref=chunk(part_ref, peer),
            dst_ref=slots.at[k - 1],
            send_sem=rs_send.at[k - 1],
            recv_sem=rs_recv.at[k - 1],
            device_id={"row": peer},
            device_id_type=MESH,
        )
        copy.start()
        scatters.append(copy)
    added = chunk(part_ref, row)[...]
    for k in range(1, n_row):
        scatters[k - 1].wait_recv()
        added = added + slots[k - 1]
    mine = chunk(total_ref, row)
    mine[...] = added
    gathers = []
    for k in range(1, n_row):
        copy = pltpu.make_async_remote_copy(
            src_ref=mine,
            dst_ref=mine,
            send_sem=ag_send.at[k - 1],
            recv_sem=ag_recv.at[k - 1],
            device_id={"row": lax.rem(row + k, n_row)},
            device_id_type=MESH,
        )
        copy.start()
        gathers.append(copy)
    for k in range(1, n_row):
        source = lax.rem(row + n_row - k, n_row)
        pltpu.make_async_remote_copy(
            src_ref=mine,
            dst_ref=chunk(total_ref, source),
            send_sem=ag_send.at[k - 1],
            recv_sem=ag_recv.at[k - 1],
            device_id={"row": source},
            device_id_type=MESH,
        ).wait_recv()

    chip, core = col // 2, lax.rem(col, 2)
    partner = col + 1 - 2 * core
    last = n_col // 2 - 1
    piece = width // pieces

    def hand(i, m, way, target):
        view = wide_ref.at[:, pl.ds(i * width + m * piece, piece)]
        return pltpu.make_async_remote_copy(
            src_ref=view,
            dst_ref=view,
            send_sem=ch_send.at[way, i, m],
            recv_sem=ch_recv.at[i, m],
            device_id={"col": target},
            device_id_type=MESH,
        )

    places = []
    for i in range(blocks):
        source = blocks * row + i
        carries = core == lax.rem(source, 2)
        start = source // 2
        up = carries & (chip >= start) & (chip < last)
        down = carries & (chip <= start) & (chip > 0)
        places.append((source, carries, start, up, down))

    def pass_on(i, m):
        _, _, _, up, down = places[i]

        @pl.when(up)
        def _():
            hand(i, m, 0, jnp.minimum(col + 2, n_col - 1)).start()

        @pl.when(down)
        def _():
            hand(i, m, 1, jnp.maximum(col - 2, 0)).start()

        hand(i, m, 2, partner).start()

    for i in range(blocks):

        @pl.when(col == places[i][0])
        def _(i=i):
            wide_ref[:, i * width : (i + 1) * width] = total_ref[...]
            for m in range(pieces):
                pass_on(i, m)

    total = total_ref[...]
    gram = dot(total, total if own else other_ref[...], ((1,), (1,)), highest)
    top = jnp.where(col == 0, total[:, B : 2 * B], 0.0)
    smalls[0] = jnp.concatenate([gram, top], axis=1)
    sends = []
    for k in range(1, n_col):
        copy = pltpu.make_async_remote_copy(
            src_ref=smalls.at[0],
            dst_ref=smalls.at[k],
            send_sem=sm_send.at[k - 1],
            recv_sem=sm_recv.at[k - 1],
            device_id={"col": lax.rem(col + k, n_col)},
            device_id_type=MESH,
        )
        copy.start()
        sends.append(copy)

    for m in range(pieces):
        for i in range(blocks):

            @pl.when(places[i][1] & (col != places[i][0]))
            def _(i=i, m=m):
                hand(i, m, 2, partner).wait_recv()
                pass_on(i, m)

    for copy in sends:
        copy.wait_recv()
    small_ref[...] = jnp.zeros_like(small_ref)

    def add_small(j, carry):
        slot = lax.rem(col + n_col - j, n_col)
        small_ref[...] += smalls[slot]
        return carry

    lax.fori_loop(0, n_col, add_small, 0)
    for i in range(blocks):
        _, carries, _, up, down = places[i]
        for m in range(pieces):

            @pl.when(jnp.logical_not(carries))
            def _(i=i, m=m):
                hand(i, m, 2, partner).wait_recv()

            @pl.when(up)
            def _(i=i, m=m):
                hand(i, m, 0, partner).wait_send()

            @pl.when(down)
            def _(i=i, m=m):
                hand(i, m, 1, partner).wait_send()

            @pl.when(carries)
            def _(i=i, m=m):
                hand(i, m, 2, partner).wait_send()

    for copy in scatters + gathers + sends:
        copy.wait_send()


def exchange(n_row, n_col, identifier, part, other=None):
    width = part.shape[1]
    blocks = n_col // n_row
    pieces = max(1, min(4, width // 256))
    lane_parts = math.gcd(n_row, width // 128)
    chunk = (B * lane_parts // n_row, width // lane_parts)
    dma = pltpu.SemaphoreType.DMA
    args = (part,) if other is None else (part, other)
    whole = pl.BlockSpec(memory_space=pltpu.VMEM)
    return pl.pallas_call(
        functools.partial(exchange_kernel, n_row, n_col, blocks, pieces, other is None),
        out_shape=(
            jax.ShapeDtypeStruct((B, width), jnp.float32),
            jax.ShapeDtypeStruct((B, blocks * width), jnp.float32),
            jax.ShapeDtypeStruct((B, 2 * B), jnp.float32),
        ),
        in_specs=[whole] * len(args),
        out_specs=(whole,) * 3,
        scratch_shapes=[
            pltpu.VMEM((n_row - 1,) + chunk, jnp.float32),
            pltpu.VMEM((n_col, B, 2 * B), jnp.float32),
            dma((n_row - 1,)),
            dma((n_row - 1,)),
            dma((n_row - 1,)),
            dma((n_row - 1,)),
            dma((n_col - 1,)),
            dma((n_col - 1,)),
            dma((3, blocks, pieces)),
            dma((blocks, pieces)),
        ],
        compiler_params=pltpu.CompilerParams(
            collective_id=identifier, has_side_effects=True, vmem_limit_bytes=24 << 20
        ),
    )(*args)


def on_device(n_row, n_col, matrix):
    rows_dev, cols_dev = matrix.shape
    first_row = lax.axis_index("row") == 0
    first_col = lax.axis_index("col") == 0
    after = first_row & (
        lax.axis_index("col") * cols_dev + jnp.arange(cols_dev, dtype=jnp.int32) >= B
    )
    share = functools.partial(exchange, n_row, n_col)
    panel_cols, panel_rows, small = share(0, jnp.where(after[None, :], matrix[:B, :], 0.0))
    small = jnp.concatenate([small[:, :B], small[:, B:].T], axis=1)
    upper, inner = factor(small)
    lower = upper.T
    basis_rows = panel_rows.at[:, B : 2 * B].add(jnp.where(first_row, lower, 0.0))
    basis_cols = panel_cols.at[:, B : 2 * B].add(jnp.where(first_col, lower, 0.0))
    image_part = dot(basis_rows, matrix, ((1,), (0,)))
    image_cols, image_rows, small = share(1, image_part, basis_cols)
    core = small[:, :B]
    middle = 0.5 * dot(inner, dot(core, inner, ((1,), (0,)), highest), ((0,), (0,)), highest)

    def updates(image, basis):
        return dot(inner, image, ((0,), (0,))) - dot(middle, basis, ((0,), (0,)))

    lefts = jnp.concatenate([basis_rows, updates(image_rows, basis_rows)], axis=0)
    rights = jnp.concatenate([updates(image_cols, basis_cols), basis_cols], axis=0)
    return matrix - dot(lefts, rights, ((0,), (0,)))


def solution(mesh):
    placed = (P("row", "col"),)
    return jax.shard_map(
        functools.partial(on_device, mesh.shape["row"], mesh.shape["col"]),
        mesh=mesh,
        in_specs=placed,
        out_specs=P("row", "col"),
        check_vma=False,
    )
```

time: 378 us -> 147 us (0.39)
  waiting for transfers between devices: 197 us -> 0 us
  Pallas kernels: 7.29 us -> 94.2 us
  blocking collectives: 50.5 us -> 0 us
  matrix products: 89.6 us -> 45.9 us
  between operations: 13.3 us -> 0.12 us
  other arithmetic: 12.3 us -> 4.42 us
    psum x3 -> x0, waiting for transfers between devices: 196 us -> none  [the longest x1 99.4 us: on_device(): image_rows = lax.psum(part_rows, 'col')]
    pallas_call x0 -> x2, Pallas kernels: none -> 86.9 us  [exchange(): pl.pallas_call(functools.partial(exchange_kernel, n_row, n_col, blocks, p...]
    psum x2 -> x0, blocking collectives: 50.5 us -> none  [the longest x1 39.6 us: on_device(): lax.psum(jnp.concatenate([core_part, edge_part], axis=1), ('row', 'col'))]
    dot_general x16 -> x8, matrix products: 89.6 us -> 45.9 us  [dot(): lax.dot_general(left, right, (dims, ((), ())), precision=precision, prefe...]
    select_n x6 -> x1, other arithmetic: 10.9 us -> 1.08 us  [on_device(): jnp.where(after[None, :], matrix[:B, :], 0.0)]
  transfers between devices with their start and end apart: 3 -> 0, of which waited for: 3 -> 0; matrix products, arithmetic and copies ran while one was open for 2% -> 0% of each run, Pallas kernels for 0% -> 0%
where the time goes in v2:
time: 147 us
  Pallas kernels  94.2 us (64%)
  matrix products  45.9 us (31%)
  other arithmetic  4.42 us (3%)
  local copies, waits for them, and re-layouts  2.12 us (1%)
    pallas_call x2, Pallas kernels, exchange(): pl.pallas_call(functools.partial(exchange_kernel, n_row, n_col, blocks, p...  86.9 us
    dot_general x8, matrix products, dot(): lax.dot_general(left, right, (dims, ((), ())), precision=precision, prefe...  45.9 us
    pallas_call x1, Pallas kernels, factor(): pl.pallas_call(factor_kernel, out_shape=(shape, shape), cost_estimate=pl....  7.28 us

profile of v2, /device:TPU:7, one launch (start us, length us, event | category | flops | bytes accessed | tf_op | source)
XLA Modules:
  0.0 146.7 jit_solution(121483462021677648)
XLA Ops:
  0.0 0.6 compare_reduce_fusion.1
  0.6 0.7 compare_reduce_fusion
  1.3 1.1 slice_select_fusion.refs_0_
  2.4 42.5 %shard_map.17 = (f32[64,2048]{1,0:T(8,128)S(1)}, f32[64,4096]{1,0:T(8,128)S(1)}, f32[64,128]{1,0:T(8,128)S(1)}) custom-call(f32[64,2048]{1,0:T(8,128)S(1)} %slice_select_fusion.refs_0_), custom_call_target="tpu_custom_call" | custom-call | tf_op jit(solution)/shard_map/pallas_call | solution.py:247
  44.9 0.1 copy.2
  45.0 0.7 pad_maximum_fusion.small_ref
  45.7 7.3 %shard_map.18 = (f32[64,64]{1,0:T(8,128)}, f32[64,64]{1,0:T(8,128)}) custom-call(f32[64,128]{1,0:T(8,128)} %pad_maximum_fusion.small_ref), custom_call_target="tpu_custom_call" | custom-call | flops 30000000 | bytes 65536 | tf_op jit(solution)/shard_map/pallas_call | solution.py:51
  53.0 0.0 copy-start
  53.0 0.8 copy.3
  53.9 1.3 add_select_fusion
  55.2 0.6 scatter-add.9.refs_1_
  55.8 0.6 scatter-add.6
  56.4 16.5 %fusion.10.refs_0_ = f32[64,2048]{1,0:T(8,128)S(1)} fusion(f32[64,4096]{1,0:T(8,128)S(1)} %scatter-add.6, f32[4096,2048]{1,0:T(8,128)} %param.5), kind=kOutput, calls=%fused_computation.23 | convolution fusion | flops 3221225472 | bytes 35127296 | tf_op jit(solution)/shard_map/dot_general | solution.py:18
  72.9 44.4 %shard_map.19 = (f32[64,2048]{1,0:T(8,128)S(1)}, f32[64,4096]{1,0:T(8,128)S(1)}, f32[64,128]{1,0:T(8,128)S(1)}) custom-call(f32[64,2048]{1,0:T(8,128)S(1)} %fusion.10.refs_0_, f32[64,2048]{1,0:T(8,128)S(1)} %scatter-add.9.refs_1_), custom_call_target="tpu_custom_call" | custom-call | tf_op jit(solution)/shard_map/pallas_call | solution.py:247
  117.3 0.0 copy-done
  117.3 0.6 fusion.11
  118.0 0.2 fusion.6
  118.1 0.2 convolution_multiply_fusion
  118.4 0.4 fusion.12
  118.8 0.4 convolution_subtract_fusion.2
  119.2 0.7 convolution_subtract_fusion.1
  119.9 26.8 %convolution_subtract_fusion = f32[4096,2048]{1,0:T(8,128)} fusion(f32[4096,2048]{1,0:T(8,128)} %param.5, f32[64,4096]{1,0:T(8,128)S(1)} %convolution_subtract_fusion.1, f32[64,4096]{1,0:T(8,128)S(1)} %scatter-add.6, f32[64,2048]{1,0:T(8,128)S(1)} %scatter-add.9.refs_1_, f32[64,2048]{1,0:T(8,128)S(1)} %convolution_subtract_fusion.2), kind=kOutput, calls=%fused_computation | convolution fusion | flops 6451625984 | bytes 70254592 | tf_op jit(solution)/shard_map/dot_general | solution.py:18
  (2 shorter events, 0.0 us)
Async XLA Ops:
  53.0 64.3 %copy-start = (f32[64,64]{1,0:T(8,128)S(1)}, f32[64,64]{1,0:T(8,128)}, u32[]{:S(2)}) copy-start(f32[64,64]{1,0:T(8,128)} %get-tuple-element.40) | copy-start | bytes 49156

commit v3 on v2

--- a/solution.py
+++ b/solution.py
@@ -238,7 +238,7 @@
 def exchange(n_row, n_col, identifier, part, other=None):
     width = part.shape[1]
     blocks = n_col // n_row
-    pieces = max(1, min(4, width // 256))
+    pieces = min(8, width // 128)
     lane_parts = math.gcd(n_row, width // 128)
     chunk = (B * lane_parts // n_row, width // lane_parts)
     dma = pltpu.SemaphoreType.DMA
@@ -271,6 +271,80 @@
     )(*args)
 
 
+def halves(values):
+    top = values.astype(jnp.bfloat16)
+    return top, (values - top.astype(jnp.float32)).astype(jnp.bfloat16)
+
+
+def image_kernel(basis_ref, matrix_ref, out_ref):
+    @pl.when(pl.program_id(0) == 0)
+    def _():
+        out_ref[...] = jnp.zeros_like(out_ref)
+
+    basis_top, basis_rest = halves(basis_ref[...])
+    top, rest = halves(matrix_ref[...])
+    both = dot(jnp.concatenate([basis_top, basis_rest], axis=0), top, ((1,), (0,)), None)
+    out_ref[...] += both[:B] + both[B:] + dot(basis_top, rest, ((1,), (0,)), None)
+
+
+def image(basis, matrix):
+    rows, cols = matrix.shape
+    tile = math.gcd(rows, 256)
+    return pl.pallas_call(
+        image_kernel,
+        grid=(rows // tile,),
+        in_specs=[
+            pl.BlockSpec((B, tile), lambda i: (0, i)),
+            pl.BlockSpec((tile, cols), lambda i: (i, 0)),
+        ],
+        out_specs=pl.BlockSpec((B, cols), lambda i: (0, 0)),
+        out_shape=jax.ShapeDtypeStruct((B, cols), jnp.float32),
+        compiler_params=pltpu.CompilerParams(vmem_limit_bytes=32 << 20),
+    )(basis, matrix)
+
+
+def reduce_kernel(
+    matrix_ref, basis_rows_ref, image_rows_ref, basis_ref, image_ref, mix_ref, out_ref, rights_ref
+):
+    def update(image, basis):
+        return dot(mix_ref[...], jnp.concatenate([image, basis], axis=0), ((0,), (0,)), highest)
+
+    @pl.when(pl.program_id(0) == 0)
+    def _():
+        basis = basis_ref[...]
+        top, rest = halves(jnp.concatenate([update(image_ref[...], basis), basis], axis=0))
+        rights_ref[...] = jnp.concatenate([top, rest, top], axis=0)
+
+    basis = basis_rows_ref[...]
+    lefts = jnp.concatenate([basis, update(image_rows_ref[...], basis)], axis=0)
+    top, rest = halves(lefts.T)
+    lefts = jnp.concatenate([top, top, rest], axis=1)
+    out_ref[...] = matrix_ref[...] - dot(lefts, rights_ref[...], ((1,), (0,)), None)
+
+
+def reduce(matrix, basis_rows, image_rows, basis_cols, image_cols, mix):
+    rows, cols = matrix.shape
+    tile = math.gcd(rows, 256)
+    strip = pl.BlockSpec((B, tile), lambda i: (0, i))
+    whole = pl.BlockSpec((B, cols), lambda i: (0, 0))
+    return pl.pallas_call(
+        reduce_kernel,
+        grid=(rows // tile,),
+        in_specs=[
+            pl.BlockSpec((tile, cols), lambda i: (i, 0)),
+            strip,
+            strip,
+            whole,
+            whole,
+            pl.BlockSpec((2 * B, B), lambda i: (0, 0)),
+        ],
+        out_specs=pl.BlockSpec((tile, cols), lambda i: (i, 0)),
+        out_shape=jax.ShapeDtypeStruct(matrix.shape, jnp.float32),
+        scratch_shapes=[pltpu.VMEM((6 * B, cols), jnp.bfloat16)],
+        compiler_params=pltpu.CompilerParams(vmem_limit_bytes=32 << 20),
+    )(matrix, basis_rows, image_rows, basis_cols, image_cols, mix)
+
+
 def on_device(n_row, n_col, matrix):
     rows_dev, cols_dev = matrix.shape
     first_row = lax.axis_index("row") == 0
@@ -285,17 +359,11 @@
     lower = upper.T
     basis_rows = panel_rows.at[:, B : 2 * B].add(jnp.where(first_row, lower, 0.0))
     basis_cols = panel_cols.at[:, B : 2 * B].add(jnp.where(first_col, lower, 0.0))
-    image_part = dot(basis_rows, matrix, ((1,), (0,)))
-    image_cols, image_rows, small = share(1, image_part, basis_cols)
+    image_cols, image_rows, small = share(1, image(basis_rows, matrix), basis_cols)
     core = small[:, :B]
     middle = 0.5 * dot(inner, dot(core, inner, ((1,), (0,)), highest), ((0,), (0,)), highest)
-
-    def updates(image, basis):
-        return dot(inner, image, ((0,), (0,))) - dot(middle, basis, ((0,), (0,)))
-
-    lefts = jnp.concatenate([basis_rows, updates(image_rows, basis_rows)], axis=0)
-    rights = jnp.concatenate([updates(image_cols, basis_cols), basis_cols], axis=0)
-    return matrix - dot(lefts, rights, ((0,), (0,)))
+    mix = jnp.concatenate([inner, -middle], axis=0)
+    return reduce(matrix, basis_rows, image_rows, basis_cols, image_cols, mix)
 
 
 def solution(mesh):

time: 147 us -> 151 us (1.027)
  Pallas kernels: 94.2 us -> 143 us
  matrix products: 45.9 us -> 0.4 us
    pallas_call x0 -> x2, Pallas kernels: none -> 53.2 us  [the longest x1 34.6 us: reduce(): pl.pallas_call(reduce_kernel, grid=(rows // tile,), in_specs=[pl.BlockSpe...]
    dot_general x8 -> x2, matrix products: 45.9 us -> 0.4 us  [dot(): lax.dot_general(left, right, (dims, ((), ())), precision=precision, prefe...]
    pallas_call x2, Pallas kernels: 86.9 us -> 83 us  [exchange(): pl.pallas_call(functools.partial(exchange_kernel, n_row, n_col, blocks, p...]
where the time goes in v3:
time: 151 us
  Pallas kernels  143 us (95%)
  other arithmetic  4.43 us (3%)
  local copies, waits for them, and re-layouts  2.12 us (1%)
    pallas_call x2, Pallas kernels, exchange(): pl.pallas_call(functools.partial(exchange_kernel, n_row, n_col, blocks, p...  83 us
    pallas_call x1, Pallas kernels, reduce(): pl.pallas_call(reduce_kernel, grid=(rows // tile,), in_specs=[pl.BlockSpe...  34.6 us
    pallas_call x1, Pallas kernels, image(): pl.pallas_call(image_kernel, grid=(rows // tile,), in_specs=[pl.BlockSpec...  18.6 us
    pallas_call x1, Pallas kernels, factor(): pl.pallas_call(factor_kernel, out_shape=(shape, shape), cost_estimate=pl....  7.28 us

profile of v3, /device:TPU:7, one launch (start us, length us, event | category | flops | bytes accessed | tf_op | source)
XLA Modules:
  0.0 150.5 jit_solution(13230172048711914468)
XLA Ops:
  0.0 0.6 compare_reduce_fusion.1
  0.6 0.7 compare_reduce_fusion
  1.3 1.1 slice_select_fusion.refs_0_
  2.4 41.6 %shard_map.17 = (f32[64,2048]{1,0:T(8,128)S(1)}, f32[64,4096]{1,0:T(8,128)S(1)}, f32[64,128]{1,0:T(8,128)S(1)}) custom-call(f32[64,2048]{1,0:T(8,128)S(1)} %slice_select_fusion.refs_0_), custom_call_target="tpu_custom_call" | custom-call | tf_op jit(solution)/shard_map/pallas_call | solution.py:247
  44.0 0.1 copy.2
  44.1 0.7 pad_maximum_fusion.1.small_ref
  44.8 7.3 %shard_map.18 = (f32[64,64]{1,0:T(8,128)}, f32[64,64]{1,0:T(8,128)}) custom-call(f32[64,128]{1,0:T(8,128)} %pad_maximum_fusion.1.small_ref), custom_call_target="tpu_custom_call" | custom-call | flops 30000000 | bytes 65536 | tf_op jit(solution)/shard_map/pallas_call | solution.py:51
  52.1 0.0 copy-start
  52.1 0.8 copy.3
  52.9 1.3 add_select_fusion
  54.3 0.6 scatter-add.9.refs_1_.basis_ref
  54.9 0.6 scatter-add.6.basis_ref.basis_rows_ref
  55.5 18.6 %shard_map.19.refs_0_ = f32[64,2048]{1,0:T(8,128)S(1)} custom-call(f32[64,4096]{1,0:T(8,128)S(1)} %scatter-add.6.basis_ref.basis_rows_ref, f32[4096,2048]{1,0:T(8,128)} %matrix_ref.3), custom_call_target="tpu_custom_call" | custom-call | tf_op jit(solution)/shard_map/pallas_call | solution.py:293
  74.0 41.4 %shard_map.20 = (f32[64,2048]{1,0:T(8,128)S(1)}, f32[64,4096]{1,0:T(8,128)S(1)}, f32[64,128]{1,0:T(8,128)S(1)}) custom-call(f32[64,2048]{1,0:T(8,128)S(1)} %shard_map.19.refs_0_, f32[64,2048]{1,0:T(8,128)S(1)} %scatter-add.9.refs_1_.basis_ref), custom_call_target="tpu_custom_call" | custom-call | tf_op jit(solution)/shard_map/pallas_call | solution.py:247
  115.5 0.0 copy-done
  115.5 0.2 fusion.1
  115.6 0.2 fusion
  115.9 34.6 %shard_map.21 = f32[4096,2048]{1,0:T(8,128)} custom-call(f32[4096,2048]{1,0:T(8,128)} %matrix_ref.3, f32[64,4096]{1,0:T(8,128)S(1)} %scatter-add.6.basis_ref.basis_rows_ref, f32[64,4096]{1,0:T(8,128)S(1)} %get-tuple-element.41.image_rows_ref, f32[64,2048]{1,0:T(8,128)S(1)} %scatter-add.9.refs_1_.basis_ref, f32[64,2048]{1,0:T(8,128)S(1)} %get-tuple-element.42.image_ref, ...), custom_call_target="tpu_custom_call" | custom-call | tf_op jit(solution)/shard_map/pallas_call | solution.py:330
  (3 shorter events, 0.0 us)
Async XLA Ops:
  52.1 63.4 %copy-start = (f32[64,64]{1,0:T(8,128)S(1)}, f32[64,64]{1,0:T(8,128)}, u32[]{:S(2)}) copy-start(f32[64,64]{1,0:T(8,128)} %get-tuple-element.43) | copy-start | bytes 49156

commit v4 on v2

--- a/solution.py
+++ b/solution.py
@@ -119,24 +119,17 @@
         )
         copy.start()
         gathers.append(copy)
-    for k in range(1, n_row):
-        source = lax.rem(row + n_row - k, n_row)
-        pltpu.make_async_remote_copy(
-            src_ref=mine,
-            dst_ref=chunk(total_ref, source),
-            send_sem=ag_send.at[k - 1],
-            recv_sem=ag_recv.at[k - 1],
-            device_id={"row": source},
-            device_id_type=MESH,
-        ).wait_recv()
-
     chip, core = col // 2, lax.rem(col, 2)
     partner = col + 1 - 2 * core
     last = n_col // 2 - 1
     piece = width // pieces
+    streamed = lane_parts == n_row and pieces == n_row
+
+    def place(m):
+        return pl.multiple_of((lax.rem(row + n_row - m, n_row) if streamed else m) * piece, piece)
 
     def hand(i, m, way, target):
-        view = wide_ref.at[:, pl.ds(i * width + m * piece, piece)]
+        view = wide_ref.at[:, pl.ds(i * width + place(m), piece)]
         return pltpu.make_async_remote_copy(
             src_ref=view,
             dst_ref=view,
@@ -168,13 +161,43 @@
 
         hand(i, m, 2, partner).start()
 
+    def begin(m):
+        for i in range(blocks):
+
+            @pl.when(col == places[i][0])
+            def _(i=i):
+                wide_ref[:, pl.ds(i * width + place(m), piece)] = total_ref[:, pl.ds(place(m), piece)]
+                pass_on(i, m)
+
+    if streamed:
+        begin(0)
+    for k in range(1, n_row):
+        source = lax.rem(row + n_row - k, n_row)
+        pltpu.make_async_remote_copy(
+            src_ref=mine,
+            dst_ref=chunk(total_ref, source),
+            send_sem=ag_send.at[k - 1],
+            recv_sem=ag_recv.at[k - 1],
+            device_id={"row": source},
+            device_id_type=MESH,
+        ).wait_recv()
+        if streamed:
+            begin(k)
+    if not streamed:
+        for m in range(pieces):
+            begin(m)
+
+    def follow(i, m, chosen):
+        @pl.when(chosen)
+        def _():
+            hand(i, m, 2, partner).wait_recv()
+            pass_on(i, m)
+
+    nearest = []
     for i in range(blocks):
-
-        @pl.when(col == places[i][0])
-        def _(i=i):
-            wide_ref[:, i * width : (i + 1) * width] = total_ref[...]
-            for m in range(pieces):
-                pass_on(i, m)
+        _, carries, start, _, _ = places[i]
+        nearest.append(carries & ((chip == start + 1) | (chip == start - 1)))
+        follow(i, 0, nearest[i])
 
     total = total_ref[...]
     gram = dot(total, total if own else other_ref[...], ((1,), (1,)), highest)
@@ -195,11 +218,8 @@
 
     for m in range(pieces):
         for i in range(blocks):
-
-            @pl.when(places[i][1] & (col != places[i][0]))
-            def _(i=i, m=m):
-                hand(i, m, 2, partner).wait_recv()
-                pass_on(i, m)
+            rest = places[i][1] & (col != places[i][0])
+            follow(i, m, rest & jnp.logical_not(nearest[i]) if m == 0 else rest)
 
     for copy in sends:
         copy.wait_recv()

time: 147 us -> 143 us (0.973)
  Pallas kernels: 94.2 us -> 90.4 us
    pallas_call x2, Pallas kernels: 86.9 us -> 83.1 us  [exchange(): pl.pallas_call(functools.partial(exchange_kernel, n_row, n_col, blocks, p...]
where the time goes in v4:
time: 143 us
  Pallas kernels  90.4 us (63%)
  matrix products  45.9 us (32%)
  other arithmetic  4.42 us (3%)
  local copies, waits for them, and re-layouts  2.12 us (1%)
    pallas_call x2, Pallas kernels, exchange(): pl.pallas_call(functools.partial(exchange_kernel, n_row, n_col, blocks, p...  83.1 us
    dot_general x8, matrix products, dot(): lax.dot_general(left, right, (dims, ((), ())), precision=precision, prefe...  45.9 us
    pallas_call x1, Pallas kernels, factor(): pl.pallas_call(factor_kernel, out_shape=(shape, shape), cost_estimate=pl....  7.28 us

profile of v4, /device:TPU:7, one launch (start us, length us, event | category | flops | bytes accessed | tf_op | source)
XLA Modules:
  0.0 143.0 jit_solution(8234869235383426617)
XLA Ops:
  0.0 0.6 compare_reduce_fusion.1
  0.6 0.7 compare_reduce_fusion
  1.3 1.1 slice_select_fusion.refs_0_
  2.4 41.9 %shard_map.17 = (f32[64,2048]{1,0:T(8,128)S(1)}, f32[64,4096]{1,0:T(8,128)S(1)}, f32[64,128]{1,0:T(8,128)S(1)}) custom-call(f32[64,2048]{1,0:T(8,128)S(1)} %slice_select_fusion.refs_0_), custom_call_target="tpu_custom_call" | custom-call | tf_op jit(solution)/shard_map/pallas_call | solution.py:267
  44.3 0.1 copy.2
  44.4 0.7 pad_maximum_fusion.small_ref
  45.1 7.3 %shard_map.18 = (f32[64,64]{1,0:T(8,128)}, f32[64,64]{1,0:T(8,128)}) custom-call(f32[64,128]{1,0:T(8,128)} %pad_maximum_fusion.small_ref), custom_call_target="tpu_custom_call" | custom-call | flops 30000000 | bytes 65536 | tf_op jit(solution)/shard_map/pallas_call | solution.py:51
  52.4 0.0 copy-start
  52.4 0.8 copy.3
  53.2 1.3 add_select_fusion
  54.5 0.6 scatter-add.9.refs_1_
  55.1 0.6 scatter-add.6
  55.8 16.6 %fusion.10.refs_0_ = f32[64,2048]{1,0:T(8,128)S(1)} fusion(f32[64,4096]{1,0:T(8,128)S(1)} %scatter-add.6, f32[4096,2048]{1,0:T(8,128)} %param.5), kind=kOutput, calls=%fused_computation.23 | convolution fusion | flops 3221225472 | bytes 35127296 | tf_op jit(solution)/shard_map/dot_general | solution.py:18
  72.3 41.3 %shard_map.19 = (f32[64,2048]{1,0:T(8,128)S(1)}, f32[64,4096]{1,0:T(8,128)S(1)}, f32[64,128]{1,0:T(8,128)S(1)}) custom-call(f32[64,2048]{1,0:T(8,128)S(1)} %fusion.10.refs_0_, f32[64,2048]{1,0:T(8,128)S(1)} %scatter-add.9.refs_1_), custom_call_target="tpu_custom_call" | custom-call | tf_op jit(solution)/shard_map/pallas_call | solution.py:267
  113.6 0.0 copy-done
  113.6 0.6 fusion.11
  114.2 0.2 fusion.6
  114.4 0.2 convolution_multiply_fusion
  114.6 0.4 fusion.12
  115.1 0.4 convolution_subtract_fusion.2
  115.5 0.7 convolution_subtract_fusion.1
  116.1 26.8 %convolution_subtract_fusion = f32[4096,2048]{1,0:T(8,128)} fusion(f32[4096,2048]{1,0:T(8,128)} %param.5, f32[64,4096]{1,0:T(8,128)S(1)} %convolution_subtract_fusion.1, f32[64,4096]{1,0:T(8,128)S(1)} %scatter-add.6, f32[64,2048]{1,0:T(8,128)S(1)} %scatter-add.9.refs_1_, f32[64,2048]{1,0:T(8,128)S(1)} %convolution_subtract_fusion.2), kind=kOutput, calls=%fused_computation | convolution fusion | flops 6451625984 | bytes 70254592 | tf_op jit(solution)/shard_map/dot_general | solution.py:18
  (2 shorter events, 0.0 us)
Async XLA Ops:
  52.4 61.2 %copy-start = (f32[64,64]{1,0:T(8,128)S(1)}, f32[64,64]{1,0:T(8,128)}, u32[]{:S(2)}) copy-start(f32[64,64]{1,0:T(8,128)} %get-tuple-element.40) | copy-start | bytes 49156

commit v5 on v4

--- a/solution.py
+++ b/solution.py
@@ -123,10 +123,12 @@
     partner = col + 1 - 2 * core
     last = n_col // 2 - 1
     piece = width // pieces
-    streamed = lane_parts == n_row and pieces == n_row
+    streamed = lane_parts == n_row and pieces == 2 * n_row
 
     def place(m):
-        return pl.multiple_of((lax.rem(row + n_row - m, n_row) if streamed else m) * piece, piece)
+        if streamed:
+            m = 2 * lax.rem(row + n_row - m // 2, n_row) + m % 2
+        return pl.multiple_of(m * piece, piece)
 
     def hand(i, m, way, target):
         view = wide_ref.at[:, pl.ds(i * width + place(m), piece)]
@@ -171,6 +173,7 @@
 
     if streamed:
         begin(0)
+        begin(1)
     for k in range(1, n_row):
         source = lax.rem(row + n_row - k, n_row)
         pltpu.make_async_remote_copy(
@@ -182,7 +185,8 @@
             device_id_type=MESH,
         ).wait_recv()
         if streamed:
-            begin(k)
+            begin(2 * k)
+            begin(2 * k + 1)
     if not streamed:
         for m in range(pieces):
             begin(m)
@@ -258,7 +262,7 @@
 def exchange(n_row, n_col, identifier, part, other=None):
     width = part.shape[1]
     blocks = n_col // n_row
-    pieces = max(1, min(4, width // 256))
+    pieces = min(2 * n_row, 8, width // 128)
     lane_parts = math.gcd(n_row, width // 128)
     chunk = (B * lane_parts // n_row, width // lane_parts)
     dma = pltpu.SemaphoreType.DMA

time: 143 us -> 141 us (0.986)
  Pallas kernels: 90.4 us -> 88 us
    pallas_call x2, Pallas kernels: 83.1 us -> 80.7 us  [exchange(): pl.pallas_call(functools.partial(exchange_kernel, n_row, n_col, blocks, p...]
where the time goes in v5:
time: 141 us
  Pallas kernels  88 us (62%)
  matrix products  45.9 us (33%)
  other arithmetic  4.42 us (3%)
  local copies, waits for them, and re-layouts  2.12 us (2%)
    pallas_call x2, Pallas kernels, exchange(): pl.pallas_call(functools.partial(exchange_kernel, n_row, n_col, blocks, p...  80.7 us
    dot_general x8, matrix products, dot(): lax.dot_general(left, right, (dims, ((), ())), precision=precision, prefe...  45.9 us
    pallas_call x1, Pallas kernels, factor(): pl.pallas_call(factor_kernel, out_shape=(shape, shape), cost_estimate=pl....  7.28 us

profile of v5, /device:TPU:7, one launch (start us, length us, event | category | flops | bytes accessed | tf_op | source)
XLA Modules:
  0.0 140.5 jit_solution(1412296986335004340)
XLA Ops:
  0.0 0.6 compare_reduce_fusion.1
  0.6 0.7 compare_reduce_fusion
  1.3 1.1 slice_select_fusion.refs_0_
  2.4 41.1 %shard_map.17 = (f32[64,2048]{1,0:T(8,128)S(1)}, f32[64,4096]{1,0:T(8,128)S(1)}, f32[64,128]{1,0:T(8,128)S(1)}) custom-call(f32[64,2048]{1,0:T(8,128)S(1)} %slice_select_fusion.refs_0_), custom_call_target="tpu_custom_call" | custom-call | tf_op jit(solution)/shard_map/pallas_call | solution.py:271
  43.6 0.1 copy.2
  43.7 0.7 pad_maximum_fusion.small_ref
  44.4 7.3 %shard_map.18 = (f32[64,64]{1,0:T(8,128)}, f32[64,64]{1,0:T(8,128)}) custom-call(f32[64,128]{1,0:T(8,128)} %pad_maximum_fusion.small_ref), custom_call_target="tpu_custom_call" | custom-call | flops 30000000 | bytes 65536 | tf_op jit(solution)/shard_map/pallas_call | solution.py:51
  51.6 0.0 copy-start
  51.6 0.8 copy.3
  52.5 1.3 add_select_fusion
  53.8 0.6 scatter-add.9.refs_1_
  54.4 0.6 scatter-add.6
  55.0 16.5 %fusion.10.refs_0_ = f32[64,2048]{1,0:T(8,128)S(1)} fusion(f32[64,4096]{1,0:T(8,128)S(1)} %scatter-add.6, f32[4096,2048]{1,0:T(8,128)} %param.5), kind=kOutput, calls=%fused_computation.23 | convolution fusion | flops 3221225472 | bytes 35127296 | tf_op jit(solution)/shard_map/dot_general | solution.py:18
  71.6 39.6 %shard_map.19 = (f32[64,2048]{1,0:T(8,128)S(1)}, f32[64,4096]{1,0:T(8,128)S(1)}, f32[64,128]{1,0:T(8,128)S(1)}) custom-call(f32[64,2048]{1,0:T(8,128)S(1)} %fusion.10.refs_0_, f32[64,2048]{1,0:T(8,128)S(1)} %scatter-add.9.refs_1_), custom_call_target="tpu_custom_call" | custom-call | tf_op jit(solution)/shard_map/pallas_call | solution.py:271
  111.1 0.0 copy-done
  111.1 0.6 fusion.11
  111.8 0.2 fusion.6
  111.9 0.2 convolution_multiply_fusion
  112.2 0.4 fusion.12
  112.6 0.4 convolution_subtract_fusion.2
  113.0 0.7 convolution_subtract_fusion.1
  113.7 26.9 %convolution_subtract_fusion = f32[4096,2048]{1,0:T(8,128)} fusion(f32[4096,2048]{1,0:T(8,128)} %param.5, f32[64,4096]{1,0:T(8,128)S(1)} %convolution_subtract_fusion.1, f32[64,4096]{1,0:T(8,128)S(1)} %scatter-add.6, f32[64,2048]{1,0:T(8,128)S(1)} %scatter-add.9.refs_1_, f32[64,2048]{1,0:T(8,128)S(1)} %convolution_subtract_fusion.2), kind=kOutput, calls=%fused_computation | convolution fusion | flops 6451625984 | bytes 70254592 | tf_op jit(solution)/shard_map/dot_general | solution.py:18
  (2 shorter events, 0.0 us)
Async XLA Ops:
  51.6 59.5 %copy-start = (f32[64,64]{1,0:T(8,128)S(1)}, f32[64,64]{1,0:T(8,128)}, u32[]{:S(2)}) copy-start(f32[64,64]{1,0:T(8,128)} %get-tuple-element.40) | copy-start | bytes 49156
